TPU v7x, 256 devices: a whole 4x4x8 slice. The times are simulated.
256 devices in a mesh: seq: 64 (over z, x, core), head: 4 (over y).
Axes of the slice: x: 4, y: 4, z: 8, core: 2. Of those that a mesh axis runs over, the one named last changes fastest.
Arguments:
- queries: bfloat16 [4, 16384, 128], P('head', 'seq'), may hold values from -8 to 8
- keys: bfloat16 [4, 16384, 128], P('head', 'seq'), may hold values from -6 to 6
- state_b: bfloat16 [4, 16384, 128], P('head', 'seq'), may hold values from -6 to 6
- state_c: bfloat16 [4, 16384, 128], P('head', 'seq'), may hold values from -6 to 6
- decay: float32 [4, 16384], P('head', 'seq'), may hold values from -1 to 0, as said below
Outputs:
- grad_b: float32 [4, 16384, 128], P('head', 'seq')
- grad_c: float32 [4, 16384, 128], P('head', 'seq')
- grad_decay: float32 [4, 16384], P('head', 'seq')
- distance: float32 [], replicated
Inputs may be any that keep to these rules, and one draw needn't show every extreme that they name: decay is negative.
All inputs are finite; a program needn't handle non-finite values.
Results may differ from a plain program's by a relative error of at most 0.00096.
Values may be sent and summed in bfloat16 or wider, within the bound.
A program may use at most 128 MiB of HBM per device.

v0:
```python
import math
import jax
import jax.numpy as jnp
from jax import lax
from jax.sharding import PartitionSpec as P

floor_score = -1e30


def prefix(part, axis, combine, identity, reverse):
    count = lax.axis_size(axis)
    place = lax.axis_index(axis)
    ahead = count - 1 - place if reverse else place
    gathered = lax.all_gather(part, axis)
    state = jnp.zeros_like(part) + jnp.asarray(identity, part.dtype)

    def one(lap, state):
        source = count - 1 - lap if reverse else lap
        return combine(state, lax.dynamic_index_in_dim(gathered, source, 0, False))

    return lax.fori_loop(0, ahead, one, state)


def score_block(query_rows, key_rows):
    return jnp.dot(query_rows, key_rows.T, preferred_element_type=jnp.float32) / math.sqrt(
        query_rows.shape[1]
    )


def pair_block(scores, causal, log_total, cum_query, cum_key, output_rows, input_rows, weight):
    attention = jnp.where(causal, jnp.exp(scores - log_total[:, None]), 0.0)
    spread = jnp.where(
        causal, jnp.exp(jnp.minimum(cum_query[:, None] - cum_key[None, :], 0.0)), 0.0
    )
    student = (
        weight * spread * jnp.dot(output_rows, input_rows.T, preferred_element_type=jnp.float32)
    )
    misfit = student - attention
    return ((misfit * spread).astype(jnp.bfloat16), misfit)


def row_max_update(state_acc, query_rows, pos_query, key_rows, pos_key):
    running_max, denominator = state_acc
    scores = score_block(query_rows, key_rows)
    causal = pos_query[:, None] >= pos_key[None, :]
    new_max = jnp.maximum(running_max, jnp.max(jnp.where(causal, scores, floor_score), axis=1))
    fresh = jnp.sum(jnp.where(causal, jnp.exp(scores - new_max[:, None]), 0.0), axis=1)
    return (new_max, denominator * jnp.exp(running_max - new_max) + fresh)


def add_terms(earlier, later):
    return earlier + later


def local(queries, keys, state_b, state_c, decay):
    query_own = queries[0]
    input_own = state_b[0]
    output_own = state_c[0]
    shard_rows = query_own.shape[0]
    state_width = input_own.shape[1]
    devices = lax.axis_size("seq")
    total_rows = shard_rows * devices
    weight = 4.0 / total_rows
    row_first = lax.axis_index("seq") * shard_rows
    row_last = row_first + shard_rows - 1
    pos_query = row_first + jnp.arange(shard_rows, dtype=jnp.int32)
    local_cum = jnp.cumsum(decay[0])
    before = prefix(local_cum[-1:], "seq", add_terms, jnp.zeros((1,), jnp.float32), False)
    cum_own = local_cum + before[0]
    cum_all = lax.all_gather(cum_own[None], "seq", axis=1, tiled=True)
    start_max = (
        jnp.full((shard_rows,), floor_score, jnp.float32),
        jnp.zeros((shard_rows,), jnp.float32),
    )
    start_pairs = (jnp.zeros((shard_rows, state_width), jnp.float32), jnp.zeros((), jnp.float32))
    key_all, input_all = (
        lax.all_gather(keys, "seq", axis=1, tiled=True),
        lax.all_gather(state_b, "seq", axis=1, tiled=True),
    )
    block_rows = math.gcd(total_rows, 1024)
    block_count = row_last // block_rows + 1

    def scan_max(block_index, state_acc):
        begin_row = block_index * block_rows
        key_rows = lax.dynamic_slice_in_dim(key_all[0], begin_row, block_rows)
        pos_key = begin_row + jnp.arange(block_rows, dtype=jnp.int32)
        return row_max_update(state_acc, query_own, pos_query, key_rows, pos_key)

    running_max, denominator = lax.fori_loop(0, block_count, scan_max, start_max)
    log_total = running_max + jnp.log(denominator)

    def tile_at(begin_row):
        key_rows = lax.dynamic_slice_in_dim(key_all[0], begin_row, block_rows)
        input_rows = lax.dynamic_slice_in_dim(input_all[0], begin_row, block_rows)
        cum_key = lax.dynamic_slice_in_dim(cum_all[0], begin_row, block_rows)
        pos_key = begin_row + jnp.arange(block_rows, dtype=jnp.int32)
        scores = score_block(query_own, key_rows)
        causal = pos_query[:, None] >= pos_key[None, :]
        mixed_tile, misfit = pair_block(
            scores, causal, log_total, cum_own, cum_key, output_own, input_rows, weight
        )
        return (mixed_tile, misfit, input_rows)

    def scan_full(block_index, state_acc):
        begin_row = block_index * block_rows
        mixed_tile, misfit, input_rows = tile_at(begin_row)
        product = jnp.dot(mixed_tile.T, output_own, preferred_element_type=jnp.float32)
        current = lax.dynamic_slice_in_dim(state_acc[2], begin_row, block_rows)
        updated = lax.dynamic_update_slice_in_dim(state_acc[2], current + product, begin_row, 0)
        return (
            state_acc[0] + jnp.dot(mixed_tile, input_rows, preferred_element_type=jnp.float32),
            state_acc[1] + jnp.sum(misfit * misfit),
            updated,
        )

    start_full = (start_pairs[0], start_pairs[1], jnp.zeros((total_rows, state_width), jnp.float32))
    grad_out, square_sum, local_grad_full = lax.fori_loop(0, block_count, scan_full, start_full)
    log_total, grad_out, square_sum, grad_full = (log_total, grad_out, square_sum, local_grad_full)
    grad_in = lax.psum_scatter(grad_full, "seq", scatter_dimension=0, tiled=True)
    cum_gradient = jnp.sum(output_own.astype(jnp.float32) * grad_out, axis=1) - jnp.sum(
        input_own.astype(jnp.float32) * grad_in, axis=1
    )
    behind = jnp.flip(jnp.cumsum(jnp.flip(cum_gradient)))
    suffix_sum = prefix(behind[:1], "seq", add_terms, jnp.zeros((1,), jnp.float32), True)
    grad_decay = ((behind + suffix_sum[0]) / math.sqrt(total_rows))[None]
    head_count = lax.axis_size("head") * queries.shape[0]
    everything = lax.psum(square_sum, ("seq", "head"))
    distance = jnp.sqrt(everything / (head_count * total_rows))
    return (grad_in[None], grad_out[None], grad_decay, distance)


def solution(mesh):
    return jax.shard_map(
        local,
        mesh=mesh,
        in_specs=(
            P("head", "seq", None),
            P("head", "seq", None),
            P("head", "seq", None),
            P("head", "seq", None),
            P("head", "seq"),
        ),
        out_specs=(P("head", "seq", None), P("head", "seq", None), P("head", "seq"), P()),
        check_vma=False,
    )
```

profile of v0, /device:TPU:8, one launch (start us, length us, event | category | flops | bytes accessed | tf_op | source)
XLA Modules:
  0.0 772.7 jit_solution(17249205068558108466)
XLA Ops:
  7.2 0.7 all-gather.7.cloned.1.call-update
  7.9 0.7 all-gather.5.cloned.1.call-update
  8.7 1.0 reduce-window.16
  9.8 1.3 dynamic-slice.4
  11.3 0.8 slice_dynamic-update-slice_fusion.1
  12.1 131.7 %all-reduce = f32[64]{0:T(128)S(1)} all-reduce(f32[64]{0:T(128)S(1)} %slice_dynamic-update-slice_fusion.1), channel_id=2, replica_groups=mesh['seq'=64,'head'=4] {'seq'}, use_global_device_ids=true, to_apply=%add | all-reduce | flops 64 | bytes 512
  143.9 117.8 %all_gather.23 = f32[1,16384]{1,0:T(1,128)S(1)} all-gather(f32[1,256]{1,0:T(1,128)S(1)} %bitcast.90), channel_id=1, replica_groups=mesh['seq'=64,'head'=4] {'seq'}, dimensions={1}, use_global_device_ids=true | all-gather | bytes 66560 | tf_op jit(solution)/shard_map/all_gather | solution.py:70
  261.6 1.6 while.52
  261.7 1.3 fusion.46
  263.4 3.5 broadcast_in_dim.40
  266.9 7.6 while.53
  266.9 1.3 fusion.55
  268.3 2.1 multiply_reduce_fusion.3
  270.4 1.3 convolution_add_fusion.3
  272.3 2.1 fusion.56
  274.5 209.6 %psum.7 = f32[]{:T(128)} all-reduce(f32[]{:T(128)} %get-tuple-element.198), channel_id=1, replica_groups=mesh['seq'=64,'head'=4] {'seq','head'}, use_global_device_ids=true, to_apply=%region_18.19 | all-reduce | flops 1 | bytes 8 | tf_op jit(solution)/shard_map/psum | solution.py:127
  484.9 73.7 %reduce-scatter.2.cloned.1.call-done = f32[256,128]{1,0:T(8,128)} async-done(((f32[16384,128]{1,0:T(8,128)}), f32[256,128]{1,0:T(8,128)}) %reduce-scatter.2.cloned.1.call-update) | async-done | bytes 131088 | tf_op jit(solution)/shard_map/reduce_scatter | solution.py:119
  558.6 1.0 fusion.26
  560.4 0.8 slice_dynamic-update-slice_fusion
  561.2 124.0 %all-reduce.1 = f32[64]{0:T(128)S(1)} all-reduce(f32[64]{0:T(128)S(1)} %slice_dynamic-update-slice_fusion), channel_id=3, replica_groups=mesh['seq'=64,'head'=4] {'seq'}, use_global_device_ids=true, to_apply=%add.1 | all-reduce | flops 64 | bytes 512
  685.2 79.2 %while.51 = (s32[]{:T(128)}, f32[1]{0:T(128)}, s32[]{:T(128)}, f32[64,1]{0,1:T(1,128)S(1)}, s32[]{:T(128)}, /*index=5*/s32[]{:T(128)}, s32[]{:T(128)}, s32[]{:T(128)}) while((s32[]{:T(128)}, f32[1]{0:T(128)}, s32[]{:T(128)}, f32[64,1]{0,1:T(1,128)S(1)}, s32[]{:T(128)}, /*index=5*/s32[]{:T(128)}, s32[]{:T(128)}, s32[]{:T(128)}) %tuple.103), condition=%wide.region_17.18_spmd, body=%wide.region_16.17_spmd.sunk | while | flops 7 | bytes 163 | solution.py:21
  687.8 0.6 constant_dynamic-slice_fusion.7
  692.8 0.6 constant_dynamic-slice_fusion.7
  706.6 0.6 constant_dynamic-slice_fusion.7
  (106 shorter events, 37.5 us)
Async XLA Ops:
  7.2 254.5 %all-gather.7.cloned.1.call-start = ((), (), s32[]{:S(2)}) async-start(), calls=%async_computation.2 | async-start | bytes 4259840 | tf_op jit(solution)/shard_map/all_gather | solution.py:77
  7.9 255.4 %all-gather.5.cloned.1.call-start = ((), (), s32[]{:S(2)}) async-start(), calls=%async_computation.1 | async-start | bytes 4259840 | tf_op jit(solution)/shard_map/all_gather | solution.py:78
  8.7 549.9 %reduce-scatter.2.cloned.1.call-start = ((), (), s32[]{:S(2)}) async-start(), calls=%async_computation.3 | async-start | bytes 8519680 | tf_op jit(solution)/shard_map/reduce_scatter | solution.py:119
  263.4 3.5 copy-start.1
  263.4 3.5 copy-start.3
  274.5 210.3 %copy-start = (f32[256,128]{1,0:T(8,128)}, f32[256,128]{1,0:T(8,128)S(1)}, u32[]{:S(2)}) copy-start(f32[256,128]{1,0:T(8,128)S(1)} %get-tuple-element.196) | copy-start | bytes 393220
  274.5 284.1 %copy-start.2 = (bf16[1,256,128]{2,1,0:T(8,128)(2,1)S(1)}, bf16[1,256,128]{2,1,0:T(8,128)(2,1)}, u32[]{:S(2)}) copy-start(bf16[1,256,128]{2,1,0:T(8,128)(2,1)} %param.15) | copy-start | bytes 196612
Sparse Core Ops, SparseCore 0:
  10.8 81.8 all-gather.6
  95.4 76.2 all-gather.4
  274.6 283.9 reduce-scatter.1
where the time goes:
time: 776 us; the launch traced here: 773 us
  blocking collectives  583 us (75%)
  waiting for transfers between devices  75.1 us (10%)
  local copies, waits for them, and re-layouts  43.8 us (6%)
  loops' own time  43.1 us (6%)
  between operations  15.7 us (2%)
  matrix products  8.2 us (1%)
    unnamed x2, blocking collectives  256 us
    psum x1, blocking collectives, local(): everything = lax.psum(square_sum, ('seq', 'head'))  210 us
    all_gather x1, blocking collectives, local(): cum_all = lax.all_gather(cum_own[None], 'seq', axis=1, tiled=True)  118 us
    reduce_scatter x1, waiting for transfers between devices, local(): lax.psum_scatter(grad_full, 'seq', scatter_dimension=0, tiled=True)  73.7 us
    another operation x2, loops' own time, prefix(): return lax.fori_loop(0, ahead, one, state)  42.4 us
    dynamic_slice x63, local copies, waits for them, and re-layouts, one(): return combine(state, lax.dynamic_index_in_dim(gathered, source, 0, False))  36.9 us
  transfers between devices with their start and end apart: 3, of which 1 were waited for; matrix products, arithmetic and copies ran while one was open for 1% of the time, Pallas kernels for 0%

commit v1 on v0

--- a/solution.py
+++ b/solution.py
@@ -67,7 +67,9 @@
     local_cum = jnp.cumsum(decay[0])
     before = prefix(local_cum[-1:], "seq", add_terms, jnp.zeros((1,), jnp.float32), False)
     cum_own = local_cum + before[0]
-    cum_all = lax.all_gather(cum_own[None], "seq", axis=1, tiled=True)
+    cum_all = jnp.concatenate(
+        lax.all_to_all(jnp.stack([cum_own[None]] * lax.axis_size("seq")), "seq", 0, 0), axis=1
+    )
     start_max = (
         jnp.full((shard_rows,), floor_score, jnp.float32),
         jnp.zeros((shard_rows,), jnp.float32),

time: 776 us -> 744 us (0.959)
  blocking collectives: 583 us -> 461 us
  starting transfers between devices: 0.11 us -> 81.1 us
  waiting for transfers between devices: 75.1 us -> 83.7 us
    all_gather x1 -> x0, blocking collectives: 118 us -> none  [local(): cum_all = lax.all_gather(cum_own[None], 'seq', axis=1, tiled=True)]
    all_to_all x0 -> x1, starting transfers between devices: none -> 81 us  [local(): lax.all_to_all(jnp.stack([cum_own[None]] * lax.axis_size('seq')), 'seq',...]
    all_to_all x0 -> x1, waiting for transfers between devices: none -> 8.25 us  [local(): lax.all_to_all(jnp.stack([cum_own[None]] * lax.axis_size('seq')), 'seq',...]
  transfers between devices with their start and end apart: 3 -> 4, of which waited for: 1 -> 2; matrix products, arithmetic and copies ran while one was open for 1% -> 1% of each run, Pallas kernels for 0% -> 0%
where the time goes in v1:
time: 744 us; the launch traced here: 741 us
  blocking collectives  461 us (62%)
  waiting for transfers between devices  83.7 us (11%)
  starting transfers between devices  81.1 us (11%)
  local copies, waits for them, and re-layouts  44.7 us (6%)
  loops' own time  43.1 us (6%)
  between operations  15.7 us (2%)
  matrix products  8.17 us (1%)
    unnamed x2, blocking collectives  256 us
    psum x1, blocking collectives, local(): everything = lax.psum(square_sum, ('seq', 'head'))  205 us
    all_to_all x1, starting transfers between devices, local(): lax.all_to_all(jnp.stack([cum_own[None]] * lax.axis_size('seq')), 'seq',...  81 us
    reduce_scatter x1, waiting for transfers between devices, local(): lax.psum_scatter(grad_full, 'seq', scatter_dimension=0, tiled=True)  74 us
    another operation x2, loops' own time, prefix(): return lax.fori_loop(0, ahead, one, state)  42.4 us
    dynamic_slice x63, local copies, waits for them, and re-layouts, one(): return combine(state, lax.dynamic_index_in_dim(gathered, source, 0, False))  36.9 us
  transfers between devices with their start and end apart: 4, of which 2 were waited for; matrix products, arithmetic and copies ran while one was open for 1% of the time, Pallas kernels for 0%

profile of v1, /device:TPU:8, one launch (start us, length us, event | category | flops | bytes accessed | tf_op | source)
XLA Modules:
  0.0 740.8 jit_solution(16685354268090047766)
XLA Ops:
  7.2 0.7 all-gather.7.cloned.1.call-update
  7.9 0.7 all-gather.5.cloned.1.call-update
  8.7 1.0 reduce-window.16
  9.8 1.3 dynamic-slice.3
  11.3 0.9 slice_dynamic-update-slice_fusion.1
  12.1 131.7 %all-reduce = f32[64]{0:T(128)S(1)} all-reduce(f32[64]{0:T(128)S(1)} %slice_dynamic-update-slice_fusion.1), channel_id=2, replica_groups=mesh['seq'=64,'head'=4] {'seq'}, use_global_device_ids=true, to_apply=%add | all-reduce | flops 64 | bytes 512
  143.8 0.7 stack.3
  144.5 81.0 %all-to-all-start = ((f32[64,1,256]{2,1,0:T(1,128)}), f32[64,1,256]{2,1,0:T(1,128)S(1)}, u32[]{:S(2)}, u32[]{:S(2)}) async-start(f32[64,1,256]{2,1,0:T(1,128)} %stack.3), calls=%async_computation | async-start | bytes 131072 | tf_op jit(solution)/shard_map/all_to_all | solution.py:71
  225.6 1.7 while.52
  225.6 1.3 fusion.46
  227.3 8.3 %all-to-all-done = f32[64,1,256]{2,1,0:T(1,128)S(1)} async-done(((f32[64,1,256]{2,1,0:T(1,128)}), f32[64,1,256]{2,1,0:T(1,128)S(1)}, u32[]{:S(2)}, u32[]{:S(2)}) %all-to-all-start) | async-done | bytes 65568 | tf_op jit(solution)/shard_map/all_to_all | solution.py:71
  235.6 3.5 broadcast_in_dim.39
  239.1 7.6 %while.53 = (s32[]{:T(128)}, f32[256,128]{1,0:T(8,128)S(1)}, f32[]{:T(128)}, f32[16384,128]{1,0:T(8,128)}, s32[]{:T(128)}, /*index=5*/f32[256]{0:T(256)S(1)}, f3...) while((s32[]{:T(128)}, f32[256,128]{1,0:T(8,128)S(1)}, ...), condition=%wide.region_10.11_spmd.clone, body=%wide.region_8.10_spmd.clone.sunk | while | flops 272532736 | bytes 5993727 | solution.py:119
  239.1 1.3 fusion.55
  240.4 2.1 multiply_reduce_fusion.3
  242.5 1.3 convolution_add_fusion.3
  244.5 2.1 fusion.56
  246.7 205.1 %psum.7 = f32[]{:T(128)} all-reduce(f32[]{:T(128)} %get-tuple-element.198), channel_id=1, replica_groups=mesh['seq'=64,'head'=4] {'seq','head'}, use_global_device_ids=true, to_apply=%region_18.19 | all-reduce | flops 1 | bytes 8 | tf_op jit(solution)/shard_map/psum | solution.py:129
  452.5 74.0 %reduce-scatter.2.cloned.1.call-done = f32[256,128]{1,0:T(8,128)} async-done(((f32[16384,128]{1,0:T(8,128)}), f32[256,128]{1,0:T(8,128)}) %reduce-scatter.2.cloned.1.call-update) | async-done | bytes 131088 | tf_op jit(solution)/shard_map/reduce_scatter | solution.py:121
  526.6 1.0 fusion.26
  528.4 0.9 slice_dynamic-update-slice_fusion
  529.3 124.0 %all-reduce.1 = f32[64]{0:T(128)S(1)} all-reduce(f32[64]{0:T(128)S(1)} %slice_dynamic-update-slice_fusion), channel_id=3, replica_groups=mesh['seq'=64,'head'=4] {'seq'}, use_global_device_ids=true, to_apply=%add.1 | all-reduce | flops 64 | bytes 512
  653.3 79.2 %while.51 = (s32[]{:T(128)}, f32[1]{0:T(128)}, s32[]{:T(128)}, f32[64,1]{0,1:T(1,128)S(1)}, s32[]{:T(128)}, /*index=5*/s32[]{:T(128)}, s32[]{:T(128)}, s32[]{:T(128)}) while((s32[]{:T(128)}, f32[1]{0:T(128)}, s32[]{:T(128)}, f32[64,1]{0,1:T(1,128)S(1)}, s32[]{:T(128)}, /*index=5*/s32[]{:T(128)}, s32[]{:T(128)}, s32[]{:T(128)}) %tuple.103), condition=%wide.region_17.18_spmd, body=%wide.region_16.17_spmd.sunk | while | flops 7 | bytes 163 | solution.py:21
  654.6 0.6 constant_dynamic-slice_fusion.5
  (107 shorter events, 38.6 us)
Async XLA Ops:
  7.2 218.4 %all-gather.7.cloned.1.call-start = ((), (), s32[]{:S(2)}) async-start(), calls=%async_computation.3 | async-start | bytes 4259840 | tf_op jit(solution)/shard_map/all_gather | solution.py:79
  7.9 227.6 %all-gather.5.cloned.1.call-start = ((), (), s32[]{:S(2)}) async-start(), calls=%async_computation.2 | async-start | bytes 4259840 | tf_op jit(solution)/shard_map/all_gather | solution.py:80
  144.5 91.0 %all-to-all-start = ((f32[64,1,256]{2,1,0:T(1,128)}), f32[64,1,256]{2,1,0:T(1,128)S(1)}, u32[]{:S(2)}, u32[]{:S(2)}) async-start(f32[64,1,256]{2,1,0:T(1,128)} %stack.3), calls=%async_computation | async-start | bytes 131072 | tf_op jit(solution)/shard_map/all_to_all | solution.py:71
  225.5 301.1 %reduce-scatter.2.cloned.1.call-start = ((), (), s32[]{:S(2)}) async-start(), calls=%async_computation.4 | async-start | bytes 8519680 | tf_op jit(solution)/shard_map/reduce_scatter | solution.py:121
  235.5 3.5 copy-start.1
  235.5 3.5 copy-start.3
  246.6 205.8 %copy-start = (f32[256,128]{1,0:T(8,128)}, f32[256,128]{1,0:T(8,128)S(1)}, u32[]{:S(2)}) copy-start(f32[256,128]{1,0:T(8,128)S(1)} %get-tuple-element.196) | copy-start | bytes 393220
  246.6 279.9 %copy-start.2 = (bf16[1,256,128]{2,1,0:T(8,128)(2,1)S(1)}, bf16[1,256,128]{2,1,0:T(8,128)(2,1)}, u32[]{:S(2)}) copy-start(bf16[1,256,128]{2,1,0:T(8,128)(2,1)} %param.15) | copy-start | bytes 196612
Sparse Core Ops, SparseCore 0:
  10.8 81.9 all-gather.6
  95.5 76.2 all-gather.4
  246.8 279.7 reduce-scatter.1
